TPU v7x, 32 devices: a whole 2x2x4 slice. The times are simulated.
32 devices in a mesh: tp: 4 (over x, core), cp: 8 (over z, y).
Axes of the slice: x: 2, y: 2, z: 4, core: 2. Of those that a mesh axis runs over, the one named last changes fastest.
Arguments:
- grad_out: bfloat16 [4, 1024, 4096], P('tp', 'cp'), may hold values from -6 to 6
- expert_ids: int32 [4, 1024, 8], P('tp', 'cp'), may hold values from 0 to 31, all different within a row; in each aligned block of 128 rows (0 to 127, 128 to 255, ..., all dimensions but the last counted through in order) at most 40 rows name the same one
- route_prob: bfloat16 [4, 1024, 8], P('tp', 'cp'), may hold values from 0.049804688 to 0.5
- attn_out: bfloat16 [4096, 4096], P('cp', 'tp'), may hold values from -0.09375 to 0.09375
- w_down: bfloat16 [32, 768, 4096], P(('tp', 'cp')), may hold values from -0.09375 to 0.09375
- hidden_saved: bfloat16 [32, 1280, 768], P(('tp', 'cp')), may hold values from -0.21875 to 0.21875
Outputs:
- grad_prob: float32 [4, 1024, 8], P('tp', 'cp')
- grad_hidden: bfloat16 [32, 1280, 768], P(('tp', 'cp'))
- grad_down: bfloat16 [32, 768, 4096], P(('tp', 'cp'))
- grad_oproj: bfloat16 [4096, 4096], P('cp', 'tp')
Inputs may be any that keep to these rules, and one draw needn't show every extreme that they name: `expert_ids`: within each device's block of 128 tokens, no expert is named by more than 40 routes, and in every draw some expert is named by exactly 40; every expert is named somewhere.
All inputs are finite; a program needn't handle non-finite values.
Results may differ from a plain program's by a relative error of at most 0.0049.
Values may be sent and summed in bfloat16 or wider, within the bound.
A program may use at most 192 MiB of HBM per device.

v0:
```python
import jax
import jax.numpy as jnp
from jax import lax
from jax.sharding import PartitionSpec as P


def local(grad_out, expert_ids, route_prob, attn_out, w_down, hidden_saved):
    tp_count = lax.axis_size("tp")
    cp_count = lax.axis_size("cp")
    n_experts = tp_count * cp_count
    slot_count = hidden_saved.shape[1]
    capacity = slot_count // n_experts
    local_rows = grad_out[0]
    token_count = local_rows.shape[0]
    width = local_rows.shape[1]
    top_count = expert_ids.shape[2]
    route_ids = expert_ids[0].reshape(-1)
    onehot = (route_ids[:, None] == jnp.arange(n_experts, dtype=jnp.int32)[None, :]).astype(
        jnp.int32
    )
    position = jnp.sum((jnp.cumsum(onehot, axis=0) - 1) * onehot, axis=1)
    target = route_ids * capacity + position
    token_of = jnp.arange(token_count * top_count, dtype=jnp.int32) // top_count
    send_rows = (
        jnp.zeros((n_experts * capacity, width), jnp.bfloat16).at[target].set(local_rows[token_of])
    )
    send_prob = (
        jnp.zeros((n_experts * capacity,), jnp.bfloat16).at[target].set(route_prob[0].reshape(-1))
    )
    got_rows, got_prob = (
        lax.all_to_all(
            send_rows.reshape(n_experts, capacity, width),
            ("tp", "cp"),
            split_axis=0,
            concat_axis=0,
            tiled=True,
        ),
        lax.all_to_all(
            send_prob.reshape(n_experts, capacity),
            ("tp", "cp"),
            split_axis=0,
            concat_axis=0,
            tiled=True,
        ),
    )
    routed = got_rows.reshape(slot_count, width)
    weight = got_prob.reshape(slot_count).astype(jnp.float32)[:, None]
    expert_weight = w_down[0]
    saved = hidden_saved[0]
    proj = lax.dot_general(
        routed, expert_weight, (((1,), (1,)), ((), ())), preferred_element_type=jnp.float32
    )
    grad_hid = (weight * proj).astype(jnp.bfloat16)
    prob_part = jnp.sum(proj * saved.astype(jnp.float32), axis=1)
    weighted = (weight * routed.astype(jnp.float32)).astype(jnp.bfloat16)
    grad_w = lax.dot_general(
        saved, weighted, (((0,), (0,)), ((), ())), preferred_element_type=jnp.float32
    ).astype(jnp.bfloat16)
    returned = lax.all_to_all(
        prob_part.reshape(n_experts, capacity),
        ("tp", "cp"),
        split_axis=0,
        concat_axis=0,
        tiled=True,
    )
    grad_prob = returned.reshape(-1)[target].reshape(1, token_count, top_count)
    gathered = lax.all_gather(grad_out, "tp", axis=0, tiled=True).reshape(-1, width)
    grad_oproj = lax.psum_scatter(
        lax.dot_general(
            gathered, attn_out, (((0,), (0,)), ((), ())), preferred_element_type=jnp.float32
        ),
        "cp",
        scatter_dimension=0,
        tiled=True,
    ).astype(jnp.bfloat16)
    return (grad_prob, grad_hid[None], grad_w[None], grad_oproj)


def solution(mesh):
    in_specs = (
        P("tp", "cp", None),
        P("tp", "cp", None),
        P("tp", "cp", None),
        P("cp", "tp"),
        P(("tp", "cp"), None, None),
        P(("tp", "cp"), None, None),
    )
    out_specs = (
        P("tp", "cp", None),
        P(("tp", "cp"), None, None),
        P(("tp", "cp"), None, None),
        P("cp", "tp"),
    )
    return jax.shard_map(local, mesh=mesh, in_specs=in_specs, out_specs=out_specs, check_vma=False)
```

profile of v0, /device:TPU:0, one launch (start us, length us, event | category | flops | bytes accessed | tf_op | source)
XLA Modules:
  0.0 526.5 jit_solution(13353454049831752493)
XLA Ops:
  7.2 0.0 copy-start
  7.2 0.0 all-gather.2.cloned.1.call-start
  7.2 0.7 all-gather.2.cloned.1.call-update
  7.9 0.0 reduce-scatter.2.cloned.1.call-start
  8.0 38.8 %all-gather.2.cloned.1.call-done = bf16[4,128,4096]{2,1,0:T(8,128)(2,1)} async-done(((bf16[1,128,4096]{2,1,0:T(8,128)(2,1)}), bf16[4,128,4096]{2,1,0:T(8,128)(2,1)}) %all-gather.2.cloned.1.call-update) | async-done | bytes 4194320 | tf_op jit(solution)/shard_map/all_gather | solution.py:67
  46.8 0.0 copy-done
  46.8 10.4 %fusion.14 = f32[4096,1024]{1,0:T(8,128)} fusion(bf16[512,4096]{1,0:T(8,128)(2,1)} %bitcast.56, bf16[512,1024]{1,0:T(8,128)(2,1)S(1)} %copy-done), kind=kOutput, calls=%fused_computation.34 | convolution fusion | flops 4294967296 | bytes 22020096 | tf_op jit(solution)/shard_map/dot_general | solution.py:69
  57.2 0.0 copy-start.4
  57.2 0.0 copy-start.5
  57.2 0.0 copy-start.2
  57.2 0.0 reduce-scatter.2.cloned.1.call-update
  57.2 0.7 copy-done.4
  57.8 0.1 copy.34
  57.9 0.1 eq.29
  58.0 0.1 eq.25
  58.1 0.0 copy-done.5
  58.1 0.1 copy.39
  58.3 0.1 reshape.176
  58.4 0.1 copy.33
  58.5 0.1 mul.41
  58.6 9.0 %reduce-window.6 = s32[32,8,128]{2,1,0:T(8,128)S(1)} reduce-window(s32[32,8,128]{2,1,0:T(8,128)S(1)} %fusion.9, s32[]{:T(128)} %constant.29.clone.1), window={size=1x1x128 pad=0_0x0_0x127_0}, to_apply=%region_0.0 | reduce-window | flops 4161536 | bytes 262148 | tf_op jit(solution)/shard_map/reduce-window
  67.6 0.1 slice.12
  67.7 0.1 copy.36
  67.9 0.1 copy.37
  67.9 0.1 add_add_fusion
  68.1 7.6 %scatter_custom_fusion.1 = bf16[1280]{0:T(1024)(128)(2,1)S(1)} fusion(s32[1024]{0:T(1024)S(1)} %bitcast.52, bf16[1024]{0:T(1024)(128)(2,1)S(1)} %reshape.176, bf16[]{:T(256)} %constant.27.clone.1), kind=kCustom, calls=%fused_computation.30 | custom fusion | bytes 2562 | tf_op jit(solution)/shard_map/scatter | solution.py:28
  75.7 0.7 all_to_all.20
  76.4 4.8 all-to-all-start.2
  81.2 0.0 copy-done.2
  81.3 7.8 %gather_fusion = bf16[1024,4096]{1,0:T(8,128)(2,1)} fusion(bf16[128,4096]{1,0:T(8,128)(2,1)S(1)} %bitcast.45, s32[1024]{0:T(1024)S(1)} %broadcast_clamp_fusion.1), kind=kCustom, calls=%fused_computation | custom fusion | bytes 16781312 | tf_op jit(solution)/shard_map/gather | solution.py:25
  89.0 18.9 %scatter_custom_fusion = bf16[1280,4096]{1,0:T(8,128)(2,1)} fusion(s32[1024]{0:T(1024)S(1)} %bitcast.53, bf16[1024,4096]{1,0:T(8,128)(2,1)} %gather_fusion, bf16[]{:T(256)} %constant.27.clone.1), kind=kCustom, calls=%fused_computation.9 | custom fusion | bytes 10486272 | tf_op jit(solution)/shard_map/scatter | solution.py:25
  107.9 0.0 all-to-all-done.2
  107.9 0.0 copy-start.3
  107.9 6.0 %all-to-all-start = ((bf16[32,40,4096]{2,1,0:T(8,128)(2,1)}), bf16[32,40,4096]{2,1,0:T(8,128)(2,1)}, u32[]{:S(2)}, u32[]{:S(2)}) async-start(bf16[32,40,4096]{2,1,0:T(8,128)(2,1)} %bitcast.46), calls=%async_computation | async-start | bytes 20971520 | tf_op jit(solution)/shard_map/all_to_all | solution.py:31
  113.9 0.0 copy-done.3
  113.9 2.3 copy.38
  116.2 0.1 convert_reduce_fusion
  116.2 0.1 reshape.146
  116.3 313.5 %all-to-all-done = bf16[32,40,4096]{2,1,0:T(8,128)(2,1)} async-done(((bf16[32,40,4096]{2,1,0:T(8,128)(2,1)}), bf16[32,40,4096]{2,1,0:T(8,128)(2,1)}, u32[]{:S(2)}, u32[]{:S(2)}) %all-to-all-start) | async-done | bytes 10485792 | tf_op jit(solution)/shard_map/all_to_all | solution.py:31
  429.8 14.8 %fusion.5 = (bf16[1,1280,768]{1,2,0:T(8,128)(2,1)}, f32[1280]{0:T(1024)S(1)}) fusion(f32[1280]{0:T(1024)S(1)} %reshape.146, bf16[1,1280,768]{1,2,0:T(8,128)(2,1)} %copy.38, bf16[1280,4096]{1,0:T(8,128)(2,1)} %bitcast.7, bf16[1,768,4096]{2,1,0:T(8,128)(2,1)} %param.10), kind=kOutput, calls=%fused_computation.13 | convolution fusion | flops 8057977856 | bytes 20719616 | tf_op jit(solution)/shard_map/dot_general | solution.py:50
  444.6 0.7 all_to_all.16
  445.3 2.5 all-to-all-start.1
  447.9 6.8 %multiply_convert_fusion = bf16[32,40,4096]{2,1,0:T(8,128)(2,1)S(1)} fusion(bf16[32,40,4096]{2,1,0:T(8,128)(2,1)} %all-to-all-done, f32[32,40]{1,0:T(8,128)S(1)} %bitcast.49), kind=kLoop, calls=%fused_computation.4 | loop fusion | flops 15728640 | bytes 20976640 | tf_op jit(solution)/shard_map/convert_element_type | solution.py:55
  454.6 11.6 %fusion.2 = bf16[1,768,4096]{1,2,0:T(8,128)(2,1)} fusion(bf16[1280,4096]{1,0:T(8,128)(2,1)S(1)} %bitcast.47, bf16[1,1280,768]{2,1,0:T(8,128)(2,1)S(1)} %copy-done.3), kind=kOutput, calls=%fused_computation.8 | convolution fusion | flops 8056209408 | bytes 18743296 | tf_op jit(solution)/shard_map/dot_general | solution.py:56
  466.2 0.0 copy-start.1
  466.2 4.1 copy.42
  470.3 8.7 %copy.43 = bf16[1,768,4096]{2,1,0:T(8,128)(2,1)} copy(bf16[1,768,4096]{1,2,0:T(8,128)(2,1)} %fusion.2) | data formatting | bytes 12582912
  478.9 0.0 all-to-all-done.1
  478.9 0.5 broadcast.139
  479.5 0.7 reduce.7
  480.2 0.1 reshape.143
  480.2 6.2 %gather_fusion.1 = f32[1024]{0:T(1024)S(1)} fusion(f32[1280]{0:T(1024)S(1)} %reshape.143, s32[1024]{0:T(1024)S(1)} %broadcast_clamp_fusion), kind=kCustom, calls=%fused_computation.1 | custom fusion | bytes 12288 | tf_op jit(solution)/shard_map/gather | solution.py:66
  486.4 0.1 reshape.144
  486.5 0.7 copy.41
  487.2 29.7 %reduce-scatter.2.cloned.1.call-done = f32[512,1024]{1,0:T(8,128)} async-done(((f32[4096,1024]{1,0:T(8,128)}), f32[512,1024]{1,0:T(8,128)}) %reduce-scatter.2.cloned.1.call-update) | async-done | bytes 2097168 | tf_op jit(solution)/shard_map/reduce_scatter | solution.py:68
  516.9 2.7 convert_element_type.58
  519.6 0.0 copy-done.1
  (10 shorter events, 0.1 us)
Async XLA Ops:
  7.2 39.6 %copy-start = (bf16[512,1024]{1,0:T(8,128)(2,1)S(1)}, bf16[512,1024]{1,0:T(8,128)(2,1)}, u32[]{:S(2)}) copy-start(bf16[512,1024]{1,0:T(8,128)(2,1)} %param.9) | copy-start | bytes 3145732
  7.2 39.6 %all-gather.2.cloned.1.call-start = ((), (), s32[]{:S(2)}) async-start(), calls=%async_computation.4 | async-start | bytes 5242880 | tf_op jit(solution)/shard_map/all_gather | solution.py:67
  7.9 509.0 %reduce-scatter.2.cloned.1.call-start = ((), (), s32[]{:S(2)}) async-start(), calls=%async_computation.5 | async-start | bytes 18874368 | tf_op jit(solution)/shard_map/reduce_scatter | solution.py:68
  57.2 0.7 copy-start.4
  57.2 1.0 copy-start.5
  57.2 24.1 %copy-start.2 = (bf16[1,128,4096]{2,1,0:T(8,128)(2,1)S(1)}, bf16[1,128,4096]{2,1,0:T(8,128)(2,1)}, u32[]{:S(2)}) copy-start(bf16[1,128,4096]{2,1,0:T(8,128)(2,1)} %param.6) | copy-start | bytes 3145732
  76.4 31.4 %all-to-all-start.2 = ((bf16[32,1,40]{2,1,0:T(2,128)(2,1)}), bf16[32,1,40]{2,1,0:T(2,128)(2,1)S(1)}, u32[]{:S(2)}, u32[]{:S(2)}) async-start(bf16[32,1,40]{2,1,0:T(2,128)(2,1)} %all_to_all.20), calls=%async_computation.2 | async-start | bytes 32768 | tf_op jit(solution)/shard_map/all_to_all | solution.py:38
  107.9 6.0 %copy-start.3 = (bf16[1,1280,768]{2,1,0:T(8,128)(2,1)S(1)}, bf16[1,1280,768]{2,1,0:T(8,128)(2,1)}, u32[]{:S(2)}) copy-start(bf16[1,1280,768]{2,1,0:T(8,128)(2,1)} %param.11) | copy-start | bytes 5898244
  107.9 321.9 %all-to-all-start = ((bf16[32,40,4096]{2,1,0:T(8,128)(2,1)}), bf16[32,40,4096]{2,1,0:T(8,128)(2,1)}, u32[]{:S(2)}, u32[]{:S(2)}) async-start(bf16[32,40,4096]{2,1,0:T(8,128)(2,1)} %bitcast.46), calls=%async_computation | async-start | bytes 20971520 | tf_op jit(solution)/shard_map/all_to_all | solution.py:31
  445.3 33.6 %all-to-all-start.1 = ((f32[32,1,40]{2,1,0:T(1,128)}), f32[32,1,40]{2,1,0:T(1,128)S(1)}, u32[]{:S(2)}, u32[]{:S(2)}) async-start(f32[32,1,40]{2,1,0:T(1,128)} %all_to_all.16), calls=%async_computation.1 | async-start | bytes 32768 | tf_op jit(solution)/shard_map/all_to_all | solution.py:59
  466.2 53.4 %copy-start.1 = (bf16[512,1024]{1,0:T(8,128)(2,1)S(1)}, bf16[512,1024]{1,0:T(8,128)(2,1)}, u32[]{:S(2)}) copy-start(bf16[512,1024]{1,0:T(8,128)(2,1)} %param.9) | copy-start | bytes 3145732
Sparse Core Ops, SparseCore 0:
  9.6 37.1 all-gather.1
  57.3 459.5 reduce-scatter.1
where the time goes:
time: 527 us; the launch traced here: 526 us
  waiting for transfers between devices  383 us (73%)
  local copies, waits for them, and re-layouts  59.8 us (11%)
  matrix products  36.7 us (7%)
  other arithmetic  19.5 us (4%)
  between operations  14.2 us (3%)
  starting transfers between devices  13.4 us (3%)
    all_to_all x1, waiting for transfers between devices, local(): lax.all_to_all(send_rows.reshape(n_experts, capacity, width), ('tp', 'cp'...  313 us
    all_gather x1, waiting for transfers between devices, local(): lax.all_gather(grad_out, 'tp', axis=0, tiled=True).reshape(-1, width)  38.8 us
    reduce_scatter x1, waiting for transfers between devices, local(): lax.psum_scatter(lax.dot_general(gathered, attn_out, (((0,), (0,)), ((),...  29.7 us
    scatter x1, local copies, waits for them, and re-layouts, local(): jnp.zeros((n_experts * capacity, width), jnp.bfloat16).at[target]  18.9 us
    unnamed x18, local copies, waits for them, and re-layouts  16.6 us
    dot_general x1, matrix products, local(): lax.dot_general(routed, expert_weight, (((1,), (1,)), ((), ())), preferre...  14.8 us
    dot_general x1, matrix products, local(): lax.dot_general(saved, weighted, (((0,), (0,)), ((), ())), preferred_elem...  11.6 us
  transfers between devices with their start and end apart: 5, of which 3 were waited for; matrix products, arithmetic and copies ran while one was open for 19% of the time, Pallas kernels for 0%

commit v1 on v0

v1 whole, which is shorter than its diff:
```python
import functools

import jax
import jax.numpy as jnp
from jax import lax
from jax.experimental import pallas as pl
from jax.experimental.pallas import tpu as pltpu
from jax.sharding import PartitionSpec as P

MESH = pl.DeviceIdType.MESH


def exchange_local(grad_out, expert_ids, route_prob, attn_out, w_down, hidden_saved):
    tp_count = lax.axis_size("tp")
    cp_count = lax.axis_size("cp")
    n_experts = tp_count * cp_count
    slot_count = hidden_saved.shape[1]
    capacity = slot_count // n_experts
    local_rows = grad_out[0]
    token_count = local_rows.shape[0]
    width = local_rows.shape[1]
    top_count = expert_ids.shape[2]
    route_ids = expert_ids[0].reshape(-1)
    onehot = (route_ids[:, None] == jnp.arange(n_experts, dtype=jnp.int32)[None, :]).astype(
        jnp.int32
    )
    position = jnp.sum((jnp.cumsum(onehot, axis=0) - 1) * onehot, axis=1)
    target = route_ids * capacity + position
    token_of = jnp.arange(token_count * top_count, dtype=jnp.int32) // top_count
    send_rows = (
        jnp.zeros((n_experts * capacity, width), jnp.bfloat16).at[target].set(local_rows[token_of])
    )
    send_prob = (
        jnp.zeros((n_experts * capacity,), jnp.bfloat16).at[target].set(route_prob[0].reshape(-1))
    )

    def swap(value):
        return lax.all_to_all(value, ("tp", "cp"), split_axis=0, concat_axis=0, tiled=True)

    routed = swap(send_rows.reshape(n_experts, capacity, width)).reshape(slot_count, width)
    got_prob = swap(send_prob.reshape(n_experts, capacity))
    weight = got_prob.reshape(slot_count).astype(jnp.float32)[:, None]
    saved = hidden_saved[0]
    proj = lax.dot_general(
        routed, w_down[0], (((1,), (1,)), ((), ())), preferred_element_type=jnp.float32
    )
    grad_hid = (weight * proj).astype(jnp.bfloat16)
    prob_part = jnp.sum(proj * saved.astype(jnp.float32), axis=1)
    weighted = (weight * routed.astype(jnp.float32)).astype(jnp.bfloat16)
    grad_w = lax.dot_general(
        saved, weighted, (((0,), (0,)), ((), ())), preferred_element_type=jnp.float32
    ).astype(jnp.bfloat16)
    returned = swap(prob_part.reshape(n_experts, capacity))
    grad_prob = returned.reshape(-1)[target].reshape(1, token_count, top_count)
    gathered = lax.all_gather(grad_out, "tp", axis=0, tiled=True).reshape(-1, width)
    grad_oproj = lax.psum_scatter(
        lax.dot_general(
            gathered, attn_out, (((0,), (0,)), ((), ())), preferred_element_type=jnp.float32
        ),
        "cp",
        scatter_dimension=0,
        tiled=True,
    ).astype(jnp.bfloat16)
    return (grad_prob, grad_hid[None], grad_w[None], grad_oproj)


def gather_kernel(n_tp, n_cp, g_ref, a_ref, gall, aall, gz_l, gz_r, gy_s, gx_s, gs_s, az_l, az_r, ay_s, g_recv, a_recv, own_sem):
    t = lax.axis_index("tp")
    c = lax.axis_index("cp")
    core = t % 2
    x = t // 2
    y = c % 2
    z = c // 2
    nz = n_cp // 2
    sib = t + 1 - 2 * core
    xt = (1 - x) * 2 + core
    yc = z * 2 + 1 - y
    has_l = z > 0
    has_r = z < nz - 1

    barrier = pltpu.get_barrier_semaphore()

    def greet(tt, cc):
        pl.semaphore_signal(barrier, inc=1, device_id=(tt, cc), device_id_type=MESH)

    greet(sib, c)
    greet(xt, c)
    greet(t, yc)

    @pl.when(has_l)
    def _():
        greet(t, c - 2)

    @pl.when(has_r)
    def _():
        greet(t, c + 2)

    pl.semaphore_wait(barrier, 3 + has_l.astype(jnp.int32) + has_r.astype(jnp.int32))

    def pick(values):
        got = values[0]
        for k in range(1, nz):
            got = jnp.where(z == k, values[k], got)
        return got

    lists = []
    for p in range(nz):
        lists.append(sorted(range(nz), key=lambda q, p=p: (abs(q - p), q)))
    order = [z] + [pick([lists[p][i] for p in range(nz)]) for i in range(1, nz)]

    def gblock(tt, zz, yy):
        return tt * n_cp + zz * 2 + yy

    def gcopy(b, src, send, dev):
        return pltpu.make_async_remote_copy(
            src_ref=src, dst_ref=gall.at[b], send_sem=send, recv_sem=g_recv.at[b], device_id=dev, device_id_type=MESH
        )

    def acopy(k, src, send, dev):
        return pltpu.make_async_remote_copy(
            src_ref=src, dst_ref=aall.at[k], send_sem=send, recv_sem=a_recv.at[k], device_id=dev, device_id_type=MESH
        )

    mine = gblock(t, z, y)
    own_g = pltpu.make_async_copy(g_ref, gall.at[mine], own_sem.at[0])
    own_a = pltpu.make_async_copy(a_ref, aall.at[c], own_sem.at[1])
    own_g.start()
    own_a.start()
    sends = []

    def line(copier, left, right, i, idx, src):
        def go(sem, dc, cond):
            op = copier(idx, src, sem.at[i], (t, c + dc))

            @pl.when(cond)
            def _():
                op.start()

            sends.append((op, cond))

        zi = order[i]
        if i == 0:
            go(left, -2, has_l)
            go(right, 2, has_r)
        else:
            go(left, -2, jnp.logical_and(zi > z, has_l))
            go(right, 2, jnp.logical_and(zi < z, has_r))

    def plain(op):
        op.start()
        sends.append((op, None))

    nx = [0]
    ns = [0]

    def to_x(b, src):
        plain(gcopy(b, src, gx_s.at[nx[0]], (xt, c)))
        nx[0] += 1

    def to_sib(b, src):
        plain(gcopy(b, src, gs_s.at[ns[0]], (sib, c)))
        ns[0] += 1

    def z_event(i):
        b = gblock(t, order[i], y)
        if i == 0:
            src = g_ref
        else:
            src = gall.at[b]
            gcopy(b, src, gy_s.at[0], (t, c)).wait_recv()
        line(gcopy, gz_l, gz_r, i, b, src)
        plain(gcopy(b, src, gy_s.at[i], (t, yc)))
        to_x(b, src)
        to_sib(b, src)

    def y_event(i):
        b = gblock(t, order[i], 1 - y)
        gcopy(b, gall.at[b], gy_s.at[0], (t, c)).wait_recv()
        to_x(b, gall.at[b])
        to_sib(b, gall.at[b])

    xseq = [(0, y)]
    for i in range(1, nz):
        xseq += [(i, y), (i - 1, 1 - y)]
    xseq.append((nz - 1, 1 - y))

    def x_event(k):
        i, yy = xseq[k]
        b = gblock(xt, order[i], yy)
        gcopy(b, gall.at[b], gy_s.at[0], (t, c)).wait_recv()
        to_sib(b, gall.at[b])

    def az_event(i):
        k = order[i] * 2 + y
        if i == 0:
            src = a_ref
        else:
            src = aall.at[k]
            acopy(k, src, ay_s.at[0], (t, c)).wait_recv()
        line(acopy, az_l, az_r, i, k, src)
        plain(acopy(k, src, ay_s.at[i], (t, yc)))

    z_event(0)
    for r in range(1, nz):
        z_event(r)
        y_event(r - 1)
        x_event(r - 1)
    az_event(0)
    y_event(nz - 1)
    x_event(nz - 1)
    for r in range(nz, 2 * nz):
        if r - nz + 1 < nz:
            az_event(r - nz + 1)
        if r >= nz + 0 and r < 2 * nz:
            if r > nz - 1 and r != nz - 1 and r < 2 * nz:
                x_event(r)
    for i in range(nz):
        k = order[i] * 2 + 1 - y
        acopy(k, aall.at[k], ay_s.at[0], (t, c)).wait_recv()

    for zz in range(nz):
        for yy in range(2):
            for xx in range(2):
                b = gblock(xx * 2 + 1 - core, zz, yy)
                gcopy(b, gall.at[b], gy_s.at[0], (t, c)).wait_recv()
    for op, cond in sends:
        if cond is None:
            op.wait_send()
        else:

            @pl.when(cond)
            def _(op=op):
                op.wait_send()

    own_g.wait()
    own_a.wait()


def gather_all(n_tp, n_cp, rows, attn):
    nz = n_cp // 2
    dma = pltpu.SemaphoreType.DMA
    n_dev = n_tp * n_cp
    return pl.pallas_call(
        functools.partial(gather_kernel, n_tp, n_cp),
        out_shape=(
            jax.ShapeDtypeStruct((n_dev,) + rows.shape, rows.dtype),
            jax.ShapeDtypeStruct((n_cp,) + attn.shape, attn.dtype),
        ),
        in_specs=[pl.BlockSpec(memory_space=pl.ANY)] * 2,
        out_specs=[pl.BlockSpec(memory_space=pl.ANY)] * 2,
        scratch_shapes=[
            dma((nz,)),
            dma((nz,)),
            dma((nz,)),
            dma((2 * nz,)),
            dma((4 * nz,)),
            dma((nz,)),
            dma((nz,)),
            dma((nz,)),
            dma((n_dev,)),
            dma((n_cp,)),
            dma((2,)),
        ],
        compiler_params=pltpu.CompilerParams(collective_id=0, has_side_effects=True),
        name="gather_rows",
    )(rows, attn)


def gather_local(grad_out, expert_ids, route_prob, attn_out, w_down, hidden_saved):
    n_tp = lax.axis_size("tp")
    n_cp = lax.axis_size("cp")
    n_dev = n_tp * n_cp
    slot_count = hidden_saved.shape[1]
    cap = slot_count // n_dev
    rows = grad_out[0]
    n_tok, width = rows.shape
    ids = expert_ids[0]
    hit = ids[None] == jnp.arange(n_dev, dtype=jnp.int32)[:, None, None]
    dense = jnp.sum(jnp.where(hit, route_prob[0].astype(jnp.float32)[None], 0.0), axis=2).astype(jnp.bfloat16)
    weights = lax.all_to_all(dense, ("tp", "cp"), split_axis=0, concat_axis=0, tiled=True)
    gall, aall = gather_all(n_tp, n_cp, rows, attn_out)

    live = weights > 0
    before = jnp.cumsum(live.astype(jnp.int32), axis=1) - 1
    take = jnp.logical_and(live[:, None, :], before[:, None, :] == jnp.arange(cap, dtype=jnp.int32)[None, :, None])
    pick = take.astype(jnp.bfloat16)
    weight = jnp.sum(jnp.where(take, weights[:, None, :].astype(jnp.float32), 0.0), axis=2).reshape(slot_count, 1)
    routed = lax.dot_general(
        pick, gall, (((2,), (1,)), ((0,), (0,))), preferred_element_type=jnp.float32
    ).astype(jnp.bfloat16).reshape(slot_count, width)
    saved = hidden_saved[0]
    proj = lax.dot_general(
        routed, w_down[0], (((1,), (1,)), ((), ())), preferred_element_type=jnp.float32
    )
    grad_hid = (weight * proj).astype(jnp.bfloat16)
    prob_part = jnp.sum(proj * saved.astype(jnp.float32), axis=1)
    weighted = (weight * routed.astype(jnp.float32)).astype(jnp.bfloat16)
    grad_w = lax.dot_general(
        saved, weighted, (((0,), (0,)), ((), ())), preferred_element_type=jnp.float32
    ).astype(jnp.bfloat16)
    part = jnp.sum(jnp.where(take, prob_part.reshape(n_dev, cap, 1), 0.0), axis=1)
    returned = lax.all_to_all(part, ("tp", "cp"), split_axis=0, concat_axis=0, tiled=True)
    grad_prob = jnp.sum(jnp.where(hit, returned[:, :, None], 0.0), axis=0)[None]

    c = lax.axis_index("cp")
    feat = width // n_cp
    mine = lax.dynamic_slice_in_dim(gall, c * feat, feat, axis=2)
    mine = mine.reshape(n_tp, n_cp, n_tok, feat)
    attn = aall.reshape(n_cp, n_tp, n_tok, attn_out.shape[1])
    grad_oproj = lax.dot_general(
        mine, attn, (((0, 1, 2), (1, 0, 2)), ((), ())), preferred_element_type=jnp.float32
    ).astype(jnp.bfloat16)
    return (grad_prob, grad_hid[None], grad_w[None], grad_oproj)


def solution(mesh):
    in_specs = (
        P("tp", "cp", None),
        P("tp", "cp", None),
        P("tp", "cp", None),
        P("cp", "tp"),
        P(("tp", "cp"), None, None),
        P(("tp", "cp"), None, None),
    )
    out_specs = (
        P("tp", "cp", None),
        P(("tp", "cp"), None, None),
        P(("tp", "cp"), None, None),
        P("cp", "tp"),
    )
    small = mesh.shape["tp"] == 4 and mesh.shape["cp"] <= 8 and mesh.shape["cp"] % 2 == 0
    local = gather_local if small else exchange_local
    return jax.shard_map(local, mesh=mesh, in_specs=in_specs, out_specs=out_specs, check_vma=False)
```

time: 527 us -> 290 us (0.55)
  waiting for transfers between devices: 383 us -> 0.01 us
  Pallas kernels: 0 us -> 190 us
  local copies, waits for them, and re-layouts: 59.8 us -> 18.6 us
  matrix products: 36.7 us -> 52.3 us
  between operations: 14.2 us -> 0.71 us
    all_to_all x3 -> x2, waiting for transfers between devices: 313 us -> 0.01 us  [the longest x1 0.01 us: gather_local(): lax.all_to_all(dense, ('tp', 'cp'), split_axis=0, concat_axis=0, tiled=True)]
    pallas_call x0 -> x1, Pallas kernels: none -> 190 us  [gather_all(): pl.pallas_call(functools.partial(gather_kernel, n_tp, n_cp), out_shape=(j...]
    all_gather x1 -> x0, waiting for transfers between devices: 38.8 us -> none  [local(): lax.all_gather(grad_out, 'tp', axis=0, tiled=True).reshape(-1, width)]
    reduce_scatter x1 -> x0, waiting for transfers between devices: 29.7 us -> none  [local(): lax.psum_scatter(lax.dot_general(gathered, attn_out, (((0,), (0,)), ((),...]
    scatter x2 -> x0, local copies, waits for them, and re-layouts: 26.4 us -> none  [the longest x1 18.9 us: local(): jnp.zeros((n_experts * capacity, width), jnp.bfloat16).at[target]]
    dot_general x3 -> x4, matrix products: 36.7 us -> 52.3 us  [the longest x1 17.1 us: gather_local(): lax.dot_general(pick, gall, (((2,), (1,)), ((0,), (0,))), preferred_eleme...]
    gather x2 -> x0, local copies, waits for them, and re-layouts: 13.9 us -> none  [the longest x1 7.75 us: local(): local_rows[token_of]]
    another operation x2, other arithmetic: 9.04 us -> 0.29 us  [gather_local(): before = jnp.cumsum(live.astype(jnp.int32), axis=1) - 1]
  transfers between devices with their start and end apart: 5 -> 2, of which waited for: 3 -> 0; matrix products, arithmetic and copies ran while one was open for 19% -> 8% of each run, Pallas kernels for 0% -> 66%
where the time goes in v1:
time: 290 us; the launch traced here: 289 us
  Pallas kernels  190 us (66%)
  matrix products  52.3 us (18%)
  local copies, waits for them, and re-layouts  18.6 us (6%)
  other arithmetic  16.7 us (6%)
  starting transfers between devices  10.9 us (4%)
    pallas_call x1, Pallas kernels, gather_all(): pl.pallas_call(functools.partial(gather_kernel, n_tp, n_cp), out_shape=(j...  190 us
    dot_general x1, matrix products, gather_local(): lax.dot_general(pick, gall, (((2,), (1,)), ((0,), (0,))), preferred_eleme...  17.1 us
    dot_general x1, matrix products, gather_local(): lax.dot_general(routed, w_down[0], (((1,), (1,)), ((), ())), preferred_el...  15.1 us
    unnamed x9, local copies, waits for them, and re-layouts  15 us
    dot_general x1, matrix products, gather_local(): lax.dot_general(saved, weighted, (((0,), (0,)), ((), ())), preferred_elem...  14.7 us
    convert_element_type x1, other arithmetic, gather_local(): weighted = (weight * routed.astype(jnp.float32)).astype(jnp.bfloat16)  11 us
    all_to_all x1, starting transfers between devices, gather_local(): lax.all_to_all(dense, ('tp', 'cp'), split_axis=0, concat_axis=0, tiled=True)  7.3 us
  transfers between devices with their start and end apart: 2, of which 0 were waited for; matrix products, arithmetic and copies ran while one was open for 8% of the time, Pallas kernels for 66%

profile of v1, /device:TPU:0, one launch (start us, length us, event | category | flops | bytes accessed | tf_op | source)
XLA Modules:
  0.0 289.0 jit_solution(9399287637306024528)
XLA Ops:
  0.6 0.7 bitcast_convert_fusion.1
  1.3 0.7 select_reduce_fusion.3
  2.1 0.6 copy.39
  2.7 7.3 %all-to-all-start = ((bf16[32,1,128]{2,1,0:T(2,128)(2,1)}), bf16[32,1,128]{2,1,0:T(2,128)(2,1)S(1)}, u32[]{:S(2)}, u32[]{:S(2)}) async-start(bf16[32,1,128]{2,1,0:T(2,128)(2,1)} %copy.39), calls=%async_computation | async-start | bytes 32768 | tf_op jit(solution)/shard_map/all_to_all | solution.py:280
  10.0 189.7 %gather_rows.1 = (bf16[32,128,4096]{2,1,0:T(8,128)(2,1)}, bf16[8,512,1024]{2,1,0:T(8,128)(2,1)}) custom-call(bf16[128,4096]{1,0:T(8,128)(2,1)} %bitcast.46, bf16[512,1024]{1,0:T(8,128)(2,1)} %a_ref.1), custom_call_target="tpu_custom_call" | custom-call | tf_op jit(solution)/shard_map/gather_rows/pallas_call | solution.py:243
  199.7 0.0 copy-start.2
  199.7 2.8 constant_dynamic-slice_fusion
  202.5 1.8 copy-done.2
  204.4 0.0 copy-start
  204.4 5.5 %bitcast_convert_fusion = bf16[512,1024]{1,0:T(8,128)(2,1)} fusion(bf16[4,8,128,512]{3,2,1,0:T(8,128)(2,1)S(1)} %bitcast.45, bf16[8,4,128,1024]{3,2,1,0:T(8,128)(2,1)S(1)} %bitcast.53), kind=kOutput, calls=%fused_computation.10 | convolution fusion | flops 4295491584 | bytes 13631488 | tf_op jit(solution)/shard_map/dot_general | solution.py:310
  209.9 0.0 copy-done
  209.9 2.3 copy.41
  212.1 0.0 all-to-all-done
  212.1 0.3 reduce_window_sum.14
  212.4 17.1 %convolution_convert_fusion = bf16[32,40,4096]{2,1,0:T(8,128)(2,1)} fusion(bf16[32,128,4096]{2,1,0:T(8,128)(2,1)} %get-tuple-element.6, s32[32,128]{1,0:T(8,128)S(1)} %broadcast_add_fusion, pred[32,128]{1,0:T(8,128)(4,1)S(1)} %get-tuple-element.31), kind=kOutput, calls=%fused_computation.3 | convolution fusion | flops 1347747840 | bytes 44060672 | tf_op jit(solution)/shard_map/dot_general | solution.py:288
  229.5 15.1 %multiply_reduce_fusion = (f32[1280]{0:T(1024)S(1)}, f32[1280,768]{0,1:T(8,128)}) fusion(bf16[1,1280,768]{1,2,0:T(8,128)(2,1)} %copy.41, bf16[1280,4096]{1,0:T(8,128)(2,1)} %bitcast.43, bf16[1,768,4096]{2,1,0:T(8,128)(2,1)} %param.10), kind=kOutput, calls=%fused_computation.9 | convolution fusion | flops 8056011776 | bytes 22680576 | tf_op jit(solution)/shard_map/dot_general | solution.py:292
  244.5 0.1 broadcast_in_dim.78
  244.7 0.9 select_reduce_fusion
  245.6 11.0 %multiply_convert_fusion = bf16[32,40,4096]{2,1,0:T(8,128)(2,1)} fusion(bf16[32,40,4096]{2,1,0:T(8,128)(2,1)} %convolution_convert_fusion, f32[32,40]{1,0:T(8,128)S(1)} %get-tuple-element.28), kind=kLoop, calls=%fused_computation | loop fusion | flops 15728640 | bytes 20976640 | tf_op jit(solution)/shard_map/convert_element_type | solution.py:297
  256.6 0.1 mul.26
  256.7 14.7 %fusion.4 = bf16[1,768,4096]{1,2,0:T(8,128)(2,1)} fusion(bf16[1280,4096]{1,0:T(8,128)(2,1)} %bitcast.44, bf16[1,1280,768]{2,1,0:T(8,128)(2,1)S(1)} %copy-done), kind=kOutput, calls=%fused_computation.7 | convolution fusion | flops 8056209408 | bytes 18743296 | tf_op jit(solution)/shard_map/dot_general | solution.py:298
  271.4 3.6 %all-to-all-start.1 = ((f32[32,1,128]{2,1,0:T(1,128)}), f32[32,1,128]{2,1,0:T(1,128)S(1)}, u32[]{:S(2)}, u32[]{:S(2)}) async-start(f32[32,1,128]{2,1,0:T(1,128)} %bitcast.8), calls=%async_computation.1 | async-start | bytes 32768 | tf_op jit(solution)/shard_map/all_to_all | solution.py:302
  275.1 2.4 fusion.5
  277.5 2.3 copy.44
  279.7 0.0 copy-start.1
  279.7 8.6 %copy.45 = bf16[1,768,4096]{2,1,0:T(8,128)(2,1)} copy(bf16[1,768,4096]{1,2,0:T(8,128)(2,1)} %fusion.4) | data formatting | bytes 12582912
  288.4 0.0 all-to-all-done.1
  288.4 0.0 copy-done.1
  288.4 0.6 select_reduce_fusion.2
  (3 shorter events, 0.0 us)
Async XLA Ops:
  2.7 209.5 %all-to-all-start = ((bf16[32,1,128]{2,1,0:T(2,128)(2,1)}), bf16[32,1,128]{2,1,0:T(2,128)(2,1)S(1)}, u32[]{:S(2)}, u32[]{:S(2)}) async-start(bf16[32,1,128]{2,1,0:T(2,128)(2,1)} %copy.39), calls=%async_computation | async-start | bytes 32768 | tf_op jit(solution)/shard_map/all_to_all | solution.py:280
  199.7 4.7 %copy-start.2 = (bf16[8,512,1024]{2,1,0:T(8,128)(2,1)S(1)}, bf16[8,512,1024]{2,1,0:T(8,128)(2,1)}, u32[]{:S(2)}) copy-start(bf16[8,512,1024]{2,1,0:T(8,128)(2,1)} %get-tuple-element.7) | copy-start | bytes 25165828
  204.4 5.5 %copy-start = (bf16[1,1280,768]{2,1,0:T(8,128)(2,1)S(1)}, bf16[1,1280,768]{2,1,0:T(8,128)(2,1)}, u32[]{:S(2)}) copy-start(bf16[1,1280,768]{2,1,0:T(8,128)(2,1)} %param.11) | copy-start | bytes 5898244
  271.4 16.9 %all-to-all-start.1 = ((f32[32,1,128]{2,1,0:T(1,128)}), f32[32,1,128]{2,1,0:T(1,128)S(1)}, u32[]{:S(2)}, u32[]{:S(2)}) async-start(f32[32,1,128]{2,1,0:T(1,128)} %bitcast.8), calls=%async_computation.1 | async-start | bytes 32768 | tf_op jit(solution)/shard_map/all_to_all | solution.py:302
  279.7 8.6 %copy-start.1 = (s32[1,128,8]{1,2,0:T(8,128)S(1)}, s32[1,128,8]{1,2,0:T(8,128)}, u32[]{:S(2)}) copy-start(s32[1,128,8]{1,2,0:T(8,128)} %param.7) | copy-start | bytes 12292

commit v2 on v1

--- a/solution.py
+++ b/solution.py
@@ -64,7 +64,12 @@
     return (grad_prob, grad_hid[None], grad_w[None], grad_oproj)
 
 
-def gather_kernel(n_tp, n_cp, g_ref, a_ref, gall, aall, gz_l, gz_r, gy_s, gx_s, gs_s, az_l, az_r, ay_s, g_recv, a_recv, own_sem):
+def gather_kernel(
+    n_tp, n_cp, g_ref, a_ref, w_ref, saved_ref, rank_ref, prob_ref,
+    gall, aall, hid_ref, gw_ref, op_ref, part_ref,
+    w_v, saved_v, acc, gw_v, hid_v, proj_v, gst, gcol, ast, oacc, o_v,
+    gz_l, gz_r, gy_s, gx_s, gs_s, az_l, az_r, ay_s, g_recv, a_recv, own_sem, in_sem, st_sem, col_sem, out_sem,
+):
     t = lax.axis_index("tp")
     c = lax.axis_index("cp")
     core = t % 2
@@ -78,6 +83,10 @@
     has_l = z > 0
     has_r = z < nz - 1
 
+    load_w = pltpu.make_async_copy(w_ref, w_v, in_sem.at[0])
+    load_saved = pltpu.make_async_copy(saved_ref, saved_v, in_sem.at[1])
+    load_w.start()
+    load_saved.start()
     barrier = pltpu.get_barrier_semaphore()
 
     def greet(tt, cc):
@@ -200,29 +209,159 @@
         line(acopy, az_l, az_r, i, k, src)
         plain(acopy(k, src, ay_s.at[i], (t, yc)))
 
+    cap2 = saved_v.shape[1]
+    n_tok, width = g_ref.shape
+    n_hid = saved_v.shape[2]
+    step = min(1024, width)
+    feat = o_v.shape[0]
+    cols = pl.ds(pl.multiple_of(c * feat, feat), feat)
+
+    def recv_g(b):
+        gcopy(b, gall.at[b], gy_s.at[0], (t, c)).wait_recv()
+
+    def experts(xx, i, first, last):
+        pairs = []
+        loads = []
+        for k in range(2):
+            tt = xx * 2 + (core if k == 0 else 1 - core)
+            p = tt * nz + order[i]
+            if k == 1:
+                recv_g(2 * p)
+                recv_g(2 * p + 1)
+            load = pltpu.make_async_copy(gall.at[pl.ds(2 * p, 2)], gst.at[k], st_sem.at[k])
+            load.start()
+            pairs.append(p)
+            loads.append(load)
+        picks, weights = [], []
+        for p in pairs:
+            slot = lax.broadcasted_iota(jnp.int32, (cap2, 2 * n_tok), 0)
+            take = slot == rank_ref[p]
+            weights.append(jnp.sum(jnp.where(take, prob_ref[p], 0.0), axis=1, keepdims=True))
+            picks.append(jnp.where(take, 1.0, 0.0).astype(jnp.bfloat16))
+        weight = jnp.concatenate(weights, axis=0)
+        hidden = jnp.concatenate([saved_v[p] for p in pairs], axis=0)
+        for load in loads:
+            load.wait()
+
+        def chunk(n, carry):
+            at = pl.ds(pl.multiple_of(n * step, step), step)
+            rows = jnp.concatenate(
+                [
+                    jnp.dot(
+                        picks[k],
+                        gst[k, :, :, at].reshape(2 * n_tok, step),
+                        preferred_element_type=jnp.float32,
+                    )
+                    for k in range(2)
+                ],
+                axis=0,
+            )
+            proj = lax.dot_general(
+                rows.astype(jnp.bfloat16), w_v[:, at], (((1,), (1,)), ((), ())), preferred_element_type=jnp.float32
+            )
+
+            @pl.when(n == 0)
+            def _():
+                proj_v[...] = proj
+
+            @pl.when(n > 0)
+            def _():
+                proj_v[...] += proj
+
+            scaled = (weight * rows).astype(jnp.bfloat16)
+            grad = lax.dot_general(hidden, scaled, (((0,), (0,)), ((), ())), preferred_element_type=jnp.float32)
+            if not first:
+                grad = acc[:, at] + grad
+            if last:
+                gw_v[:, at] = grad.astype(jnp.bfloat16)
+            else:
+                acc[:, at] = grad
+            return carry
+
+        lax.fori_loop(0, width // step, chunk, 0)
+        proj = proj_v[...]
+        hid = (weight * proj).astype(jnp.bfloat16)
+        sums = jnp.sum(proj * hidden.astype(jnp.float32), axis=1, keepdims=True)
+        for k, p in enumerate(pairs):
+            hid_v[p] = hid[k * cap2 : (k + 1) * cap2]
+            take = lax.broadcasted_iota(jnp.int32, (cap2, 2 * n_tok), 0) == rank_ref[p]
+            part_ref[p] = jnp.sum(
+                jnp.where(take, sums[k * cap2 : (k + 1) * cap2], 0.0), axis=0, keepdims=True
+            )
+
+    def outer(i, first):
+        zi = order[i]
+        loads = [pltpu.make_async_copy(aall.at[pl.ds(2 * zi, 2)], ast, col_sem.at[2 * n_tp])]
+        for yy in range(2):
+            for tt in range(n_tp):
+                k = yy * n_tp + tt
+                loads.append(
+                    pltpu.make_async_copy(gall.at[gblock(tt, zi, yy), :, cols], gcol.at[k], col_sem.at[k])
+                )
+        for load in loads:
+            load.start()
+        for load in loads:
+            load.wait()
+        got = lax.dot_general(
+            gcol[...].reshape(2 * n_tp * n_tok, feat),
+            ast[...].reshape(2 * n_tp * n_tok, ast.shape[2]),
+            (((0,), (0,)), ((), ())),
+            preferred_element_type=jnp.float32,
+        )
+        if first:
+            oacc[...] = got
+        else:
+            oacc[...] += got
+
+    def ay_event(i):
+        k = order[i] * 2 + 1 - y
+        acopy(k, aall.at[k], ay_s.at[0], (t, c)).wait_recv()
+
+    xo = 1 - x
     z_event(0)
+    own_g.wait()
+    own_a.wait()
+    load_w.wait()
+    load_saved.wait()
     for r in range(1, nz):
         z_event(r)
         y_event(r - 1)
         x_event(r - 1)
-    az_event(0)
+        if r == nz - 1:
+            az_event(0)
+        experts(x, r - 1, r == 1, False)
     y_event(nz - 1)
     x_event(nz - 1)
-    for r in range(nz, 2 * nz):
-        if r - nz + 1 < nz:
-            az_event(r - nz + 1)
-        if r >= nz + 0 and r < 2 * nz:
-            if r > nz - 1 and r != nz - 1 and r < 2 * nz:
-                x_event(r)
-    for i in range(nz):
-        k = order[i] * 2 + 1 - y
-        acopy(k, aall.at[k], ay_s.at[0], (t, c)).wait_recv()
-
-    for zz in range(nz):
-        for yy in range(2):
-            for xx in range(2):
-                b = gblock(xx * 2 + 1 - core, zz, yy)
-                gcopy(b, gall.at[b], gy_s.at[0], (t, c)).wait_recv()
+    az_event(1)
+    experts(x, nz - 1, False, False)
+    experts(xo, 0, False, False)
+    x_event(nz)
+    for i in range(2, nz):
+        az_event(i)
+    ay_event(0)
+    experts(xo, 1, False, False)
+    outer(0, True)
+    x_event(nz + 1)
+    ay_event(1)
+    outer(1, False)
+    x_event(nz + 2)
+    experts(xo, 2, False, False)
+    ay_event(2)
+    outer(2, False)
+    x_event(nz + 3)
+    experts(xo, 3, False, True)
+    out_gw = pltpu.make_async_copy(gw_v, gw_ref, out_sem.at[0])
+    out_gw.start()
+    out_hid = pltpu.make_async_copy(hid_v, hid_ref, out_sem.at[1])
+    out_hid.start()
+    ay_event(3)
+    outer(3, False)
+    o_v[...] = oacc[...].astype(jnp.bfloat16)
+    out_op = pltpu.make_async_copy(o_v, op_ref, out_sem.at[2])
+    out_op.start()
+    out_gw.wait()
+    out_hid.wait()
+    out_op.wait()
     for op, cond in sends:
         if cond is None:
             op.wait_send()
@@ -232,23 +371,46 @@
             def _(op=op):
                 op.wait_send()
 
-    own_g.wait()
-    own_a.wait()
-
-
-def gather_all(n_tp, n_cp, rows, attn):
+
+def gather_all(n_tp, n_cp, rows, attn, w_down, saved, rank, prob):
     nz = n_cp // 2
     dma = pltpu.SemaphoreType.DMA
     n_dev = n_tp * n_cp
+    n_tok, width = rows.shape
+    n_hid = w_down.shape[0]
+    feat = width // n_cp
+    heads = attn.shape[1]
+    slots = saved.shape[0] * saved.shape[1]
+    hbm = pl.BlockSpec(memory_space=pl.ANY)
+    vmem = pl.BlockSpec(memory_space=pltpu.VMEM)
+    shape = jax.ShapeDtypeStruct
+    bf16, f32 = jnp.bfloat16, jnp.float32
+    cap2 = saved.shape[1]
+    flops = 4 * slots * width * n_hid + 2 * n_dev * n_tok * feat * heads
     return pl.pallas_call(
         functools.partial(gather_kernel, n_tp, n_cp),
         out_shape=(
-            jax.ShapeDtypeStruct((n_dev,) + rows.shape, rows.dtype),
-            jax.ShapeDtypeStruct((n_cp,) + attn.shape, attn.dtype),
+            shape((n_dev,) + rows.shape, bf16),
+            shape((n_cp,) + attn.shape, bf16),
+            shape(saved.shape, bf16),
+            shape(w_down.shape, bf16),
+            shape((feat, heads), bf16),
+            shape(prob.shape, f32),
         ),
-        in_specs=[pl.BlockSpec(memory_space=pl.ANY)] * 2,
-        out_specs=[pl.BlockSpec(memory_space=pl.ANY)] * 2,
+        in_specs=[hbm] * 4 + [vmem] * 2,
+        out_specs=[hbm] * 5 + [vmem],
         scratch_shapes=[
+            pltpu.VMEM(w_down.shape, bf16),
+            pltpu.VMEM(saved.shape, bf16),
+            pltpu.VMEM(w_down.shape, f32),
+            pltpu.VMEM(w_down.shape, bf16),
+            pltpu.VMEM(saved.shape, bf16),
+            pltpu.VMEM((2 * cap2, n_hid), f32),
+            pltpu.VMEM((2, 2, n_tok, width), bf16),
+            pltpu.VMEM((2 * n_tp, n_tok, feat), bf16),
+            pltpu.VMEM((2,) + attn.shape, bf16),
+            pltpu.VMEM((feat, heads), f32),
+            pltpu.VMEM((feat, heads), bf16),
             dma((nz,)),
             dma((nz,)),
             dma((nz,)),
@@ -260,10 +422,17 @@
             dma((n_dev,)),
             dma((n_cp,)),
             dma((2,)),
+            dma((2,)),
+            dma((2,)),
+            dma((2 * n_tp + 1,)),
+            dma((3,)),
         ],
-        compiler_params=pltpu.CompilerParams(collective_id=0, has_side_effects=True),
-        name="gather_rows",
-    )(rows, attn)
+        compiler_params=pltpu.CompilerParams(
+            collective_id=0, has_side_effects=True, vmem_limit_bytes=56 * 1024 * 1024
+        ),
+        cost_estimate=pl.CostEstimate(flops=flops, bytes_accessed=4 * n_dev * n_tok * width, transcendentals=0),
+        name="gather_and_multiply",
+    )(rows, attn, w_down, saved, rank, prob)
 
 
 def gather_local(grad_out, expert_ids, route_prob, attn_out, w_down, hidden_saved):
@@ -278,39 +447,19 @@
     hit = ids[None] == jnp.arange(n_dev, dtype=jnp.int32)[:, None, None]
     dense = jnp.sum(jnp.where(hit, route_prob[0].astype(jnp.float32)[None], 0.0), axis=2).astype(jnp.bfloat16)
     weights = lax.all_to_all(dense, ("tp", "cp"), split_axis=0, concat_axis=0, tiled=True)
-    gall, aall = gather_all(n_tp, n_cp, rows, attn_out)
-
     live = weights > 0
-    before = jnp.cumsum(live.astype(jnp.int32), axis=1) - 1
-    take = jnp.logical_and(live[:, None, :], before[:, None, :] == jnp.arange(cap, dtype=jnp.int32)[None, :, None])
-    pick = take.astype(jnp.bfloat16)
-    weight = jnp.sum(jnp.where(take, weights[:, None, :].astype(jnp.float32), 0.0), axis=2).reshape(slot_count, 1)
-    routed = lax.dot_general(
-        pick, gall, (((2,), (1,)), ((0,), (0,))), preferred_element_type=jnp.float32
-    ).astype(jnp.bfloat16).reshape(slot_count, width)
-    saved = hidden_saved[0]
-    proj = lax.dot_general(
-        routed, w_down[0], (((1,), (1,)), ((), ())), preferred_element_type=jnp.float32
-    )
-    grad_hid = (weight * proj).astype(jnp.bfloat16)
-    prob_part = jnp.sum(proj * saved.astype(jnp.float32), axis=1)
-    weighted = (weight * routed.astype(jnp.float32)).astype(jnp.bfloat16)
-    grad_w = lax.dot_general(
-        saved, weighted, (((0,), (0,)), ((), ())), preferred_element_type=jnp.float32
-    ).astype(jnp.bfloat16)
-    part = jnp.sum(jnp.where(take, prob_part.reshape(n_dev, cap, 1), 0.0), axis=1)
-    returned = lax.all_to_all(part, ("tp", "cp"), split_axis=0, concat_axis=0, tiled=True)
+    earlier = jnp.triu(jnp.ones((n_tok, n_tok), jnp.bfloat16), 1)
+    before = jnp.dot(live.astype(jnp.bfloat16), earlier, preferred_element_type=jnp.float32).astype(jnp.int32)
+    offset = (jnp.arange(n_dev, dtype=jnp.int32) % 2 * cap)[:, None]
+    rank = jnp.where(live, before + offset, -1).reshape(n_dev // 2, 1, 2 * n_tok)
+    prob = weights.astype(jnp.float32).reshape(n_dev // 2, 1, 2 * n_tok)
+    saved = hidden_saved[0].reshape(n_dev // 2, 2 * cap, hidden_saved.shape[2])
+    _, _, hid, grad_w, grad_oproj, part = gather_all(
+        n_tp, n_cp, rows, attn_out, w_down[0], saved, rank, prob
+    )
+    returned = lax.all_to_all(part.reshape(n_dev, n_tok), ("tp", "cp"), split_axis=0, concat_axis=0, tiled=True)
     grad_prob = jnp.sum(jnp.where(hit, returned[:, :, None], 0.0), axis=0)[None]
-
-    c = lax.axis_index("cp")
-    feat = width // n_cp
-    mine = lax.dynamic_slice_in_dim(gall, c * feat, feat, axis=2)
-    mine = mine.reshape(n_tp, n_cp, n_tok, feat)
-    attn = aall.reshape(n_cp, n_tp, n_tok, attn_out.shape[1])
-    grad_oproj = lax.dot_general(
-        mine, attn, (((0, 1, 2), (1, 0, 2)), ((), ())), preferred_element_type=jnp.float32
-    ).astype(jnp.bfloat16)
-    return (grad_prob, grad_hid[None], grad_w[None], grad_oproj)
+    return (grad_prob, hid.reshape(hidden_saved.shape), grad_w[None], grad_oproj)
 
 
 def solution(mesh):
@@ -328,6 +477,6 @@
         P(("tp", "cp"), None, None),
         P("cp", "tp"),
     )
-    small = mesh.shape["tp"] == 4 and mesh.shape["cp"] <= 8 and mesh.shape["cp"] % 2 == 0
+    small = mesh.shape["tp"] == 4 and mesh.shape["cp"] == 8
     local = gather_local if small else exchange_local
     return jax.shard_map(local, mesh=mesh, in_specs=in_specs, out_specs=out_specs, check_vma=False)

time: 290 us -> 309 us (1.066)
  Pallas kernels: 190 us -> 270 us
  matrix products: 52.3 us -> 0.74 us
  waiting for transfers between devices: 0.01 us -> 14.1 us
  other arithmetic: 16.7 us -> 2.67 us
  local copies, waits for them, and re-layouts: 18.6 us -> 10.9 us
    pallas_call x1, Pallas kernels: 190 us -> 270 us  [gather_all(): pl.pallas_call(functools.partial(gather_kernel, n_tp, n_cp), out_shape=(s...]
    dot_general x4 -> x1, matrix products: 52.3 us -> 0.74 us  [gather_local(): jnp.dot(live.astype(jnp.bfloat16), earlier, preferred_element_type=jnp.fl...]
    convert_element_type x1, other arithmetic: 11 us -> 0.62 us  [gather_local(): prob = weights.astype(jnp.float32).reshape(n_dev // 2, 1, 2 * n_tok)]
    all_to_all x1, waiting for transfers between devices: 0.01 us -> 7.12 us  [gather_local(): lax.all_to_all(part.reshape(n_dev, n_tok), ('tp', 'cp'), split_axis=0, co...]
    all_to_all x1, waiting for transfers between devices: 0.01 us -> 7.03 us  [gather_local(): lax.all_to_all(dense, ('tp', 'cp'), split_axis=0, concat_axis=0, tiled=True)]
    unnamed x9 -> x7, local copies, waits for them, and re-layouts: 15 us -> 10.3 us
  transfers between devices with their start and end apart: 2 -> 2, of which waited for: 0 -> 2; matrix products, arithmetic and copies ran while one was open for 8% -> 0% of each run, Pallas kernels for 66% -> 0%
where the time goes in v2:
time: 309 us
  Pallas kernels  270 us (87%)
  waiting for transfers between devices  14.1 us (5%)
  local copies, waits for them, and re-layouts  10.9 us (4%)
  starting transfers between devices  9.77 us (3%)
    pallas_call x1, Pallas kernels, gather_all(): pl.pallas_call(functools.partial(gather_kernel, n_tp, n_cp), out_shape=(s...  270 us
    unnamed x7, local copies, waits for them, and re-layouts  10.3 us
    all_to_all x1, starting transfers between devices, gather_local(): lax.all_to_all(dense, ('tp', 'cp'), split_axis=0, concat_axis=0, tiled=True)  7.3 us
    all_to_all x1, waiting for transfers between devices, gather_local(): lax.all_to_all(part.reshape(n_dev, n_tok), ('tp', 'cp'), split_axis=0, co...  7.12 us
    all_to_all x1, waiting for transfers between devices, gather_local(): lax.all_to_all(dense, ('tp', 'cp'), split_axis=0, concat_axis=0, tiled=True)  7.03 us
  transfers between devices with their start and end apart: 2, of which 2 were waited for; matrix products, arithmetic and copies ran while one was open for 0% of the time, Pallas kernels for 0%

profile of v2, /device:TPU:0, one launch (start us, length us, event | category | flops | bytes accessed | tf_op | source)
XLA Modules:
  0.0 308.7 jit_solution(8394330705324385513)
XLA Ops:
  0.6 0.7 bitcast_convert_fusion
  1.3 0.7 select_reduce_fusion.1
  2.1 0.6 copy.21
  2.7 7.3 %all-to-all-start = ((bf16[32,1,128]{2,1,0:T(2,128)(2,1)}), bf16[32,1,128]{2,1,0:T(2,128)(2,1)S(1)}, u32[]{:S(2)}, u32[]{:S(2)}) async-start(bf16[32,1,128]{2,1,0:T(2,128)(2,1)} %copy.21), calls=%async_computation | async-start | bytes 32768 | tf_op jit(solution)/shard_map/all_to_all | solution.py:449
  10.0 7.0 %all-to-all-done = bf16[32,1,128]{2,1,0:T(2,128)(2,1)S(1)} async-done(((bf16[32,1,128]{2,1,0:T(2,128)(2,1)}), bf16[32,1,128]{2,1,0:T(2,128)(2,1)S(1)}, u32[]{:S(2)}, u32[]{:S(2)}) %all-to-all-start) | async-done | bytes 8224 | tf_op jit(solution)/shard_map/all_to_all | solution.py:449
  17.0 0.6 convert.3.prob_ref
  17.6 0.7 fusion.1
  18.4 0.0 copy-start.1
  18.4 269.8 %gather_and_multiply.1 = (bf16[32,128,4096]{2,1,0:T(8,128)(2,1)}, bf16[8,512,1024]{2,1,0:T(8,128)(2,1)}, bf16[16,80,768]{2,1,0:T(8,128)(2,1)}, bf16[768,4096]{1,...) custom-call(bf16[128,4096]{1,0:T(8,128)(2,1)} %bitcast.34, bf16[512,1024]{1,0:T(8,128)(2,1)} %a_ref.1, ...), custom_call_target="tpu_custom_call" | custom-call | flops 20401094656 | bytes 67108864 | tf_op jit(solution)/shard_map/gather_and_multiply/pallas_call | solution.py:390
  288.2 2.5 all-to-all-start.1
  290.7 7.1 %all-to-all-done.1 = f32[32,1,128]{2,1,0:T(1,128)S(1)} async-done(((f32[32,1,128]{2,1,0:T(1,128)}), f32[32,1,128]{2,1,0:T(1,128)S(1)}, u32[]{:S(2)}, u32[]{:S(2)}) %all-to-all-start.1) | async-done | bytes 16416 | tf_op jit(solution)/shard_map/all_to_all | solution.py:460
  297.8 0.0 copy-done.1
  297.8 0.6 select_reduce_fusion
  298.5 2.9 copy.31
  301.4 0.0 copy-start
  301.4 6.4 %copy.32 = bf16[1,768,4096]{2,1,0:T(8,128)(2,1)} copy(bf16[1,768,4096]{2,1,0:T(8,128)(2,1)} %bitcast.23) | data formatting | bytes 12582912
  307.8 0.0 copy-done
  307.8 1.0 copy.33
  (1 shorter events, 0.0 us)
Async XLA Ops:
  2.7 14.3 %all-to-all-start = ((bf16[32,1,128]{2,1,0:T(2,128)(2,1)}), bf16[32,1,128]{2,1,0:T(2,128)(2,1)S(1)}, u32[]{:S(2)}, u32[]{:S(2)}) async-start(bf16[32,1,128]{2,1,0:T(2,128)(2,1)} %copy.21), calls=%async_computation | async-start | bytes 32768 | tf_op jit(solution)/shard_map/all_to_all | solution.py:449
  18.4 279.4 %copy-start.1 = (s32[1,128,8]{1,2,0:T(8,128)S(1)}, s32[1,128,8]{1,2,0:T(8,128)}, u32[]{:S(2)}) copy-start(s32[1,128,8]{1,2,0:T(8,128)} %param.7) | copy-start | bytes 12292
  288.2 9.6 %all-to-all-start.1 = ((f32[32,1,128]{2,1,0:T(1,128)}), f32[32,1,128]{2,1,0:T(1,128)S(1)}, u32[]{:S(2)}, u32[]{:S(2)}) async-start(f32[32,1,128]{2,1,0:T(1,128)} %bitcast.28), calls=%async_computation.1 | async-start | bytes 32768 | tf_op jit(solution)/shard_map/all_to_all | solution.py:460
  301.4 6.4 %copy-start = (bf16[512,1024]{1,0:T(8,128)(2,1)S(1)}, bf16[512,1024]{1,0:T(8,128)(2,1)}, u32[]{:S(2)}) copy-start(bf16[512,1024]{1,0:T(8,128)(2,1)} %get-tuple-element.19) | copy-start | bytes 3145732

commit v3 on v2

--- a/solution.py
+++ b/solution.py
@@ -65,10 +65,10 @@
 
 
 def gather_kernel(
-    n_tp, n_cp, g_ref, a_ref, w_ref, saved_ref, rank_ref, prob_ref,
+    n_tp, n_cp, g_ref, a_ref, w_ref, saved_ref,
     gall, aall, hid_ref, gw_ref, op_ref, part_ref,
-    w_v, saved_v, acc, gw_v, hid_v, proj_v, gst, gcol, ast, oacc, o_v,
-    gz_l, gz_r, gy_s, gx_s, gs_s, az_l, az_r, ay_s, g_recv, a_recv, own_sem, in_sem, st_sem, col_sem, out_sem,
+    w_v, saved_v, acc, gw_v, hid_v, proj_v, gst, gcol, ast, oacc, o_v, rows_v, hidt_v, rank_v, prob_v,
+    gz_l, gz_r, gy_s, gx_s, gs_s, az_l, az_r, ay_s, g_recv, a_recv, own_sem, in_sem, st_sem, col_sem, out_sem, gw_sem,
 ):
     t = lax.axis_index("tp")
     c = lax.axis_index("cp")
@@ -210,84 +210,100 @@
         plain(acopy(k, src, ay_s.at[i], (t, yc)))
 
     cap2 = saved_v.shape[1]
-    n_tok, width = g_ref.shape
-    n_hid = saved_v.shape[2]
+    n_tok = g_ref.shape[0]
+    width = w_v.shape[1]
     step = min(1024, width)
     feat = o_v.shape[0]
     cols = pl.ds(pl.multiple_of(c * feat, feat), feat)
+    f32, bf16 = jnp.float32, jnp.bfloat16
+    nt = (((1,), (1,)), ((), ()))
 
     def recv_g(b):
         gcopy(b, gall.at[b], gy_s.at[0], (t, c)).wait_recv()
 
-    def experts(xx, i, first, last):
-        pairs = []
+    def pair_of(xx, i, k):
+        return (xx * 2 + (core if k == 0 else 1 - core)) * nz + order[i]
+
+    def taken(p):
+        return lax.broadcasted_iota(jnp.int32, (cap2, 2 * n_tok), 0) == rank_v[p][0:1]
+
+    def select(xx, i):
+        pairs = [pair_of(xx, i, k) for k in range(2)]
         loads = []
-        for k in range(2):
-            tt = xx * 2 + (core if k == 0 else 1 - core)
-            p = tt * nz + order[i]
+        for k, p in enumerate(pairs):
             if k == 1:
                 recv_g(2 * p)
                 recv_g(2 * p + 1)
             load = pltpu.make_async_copy(gall.at[pl.ds(2 * p, 2)], gst.at[k], st_sem.at[k])
             load.start()
-            pairs.append(p)
             loads.append(load)
-        picks, weights = [], []
-        for p in pairs:
-            slot = lax.broadcasted_iota(jnp.int32, (cap2, 2 * n_tok), 0)
-            take = slot == rank_ref[p]
-            weights.append(jnp.sum(jnp.where(take, prob_ref[p], 0.0), axis=1, keepdims=True))
-            picks.append(jnp.where(take, 1.0, 0.0).astype(jnp.bfloat16))
-        weight = jnp.concatenate(weights, axis=0)
-        hidden = jnp.concatenate([saved_v[p] for p in pairs], axis=0)
-        for load in loads:
-            load.wait()
+        lanes = g_ref.shape[1] - width
+        expert = t * n_cp + c
+        one = jnp.where(lax.broadcasted_iota(jnp.int32, (8, lanes), 1) == expert, 1.0, 0.0).astype(bf16)
+        row = lax.broadcasted_iota(jnp.int32, (2 * n_tok, 2 * n_tok), 0)
+        col = lax.broadcasted_iota(jnp.int32, (2 * n_tok, 2 * n_tok), 1)
+        same = (row >= n_tok) == (col >= n_tok)
+        earlier = jnp.where(jnp.logical_and(same, row < col), 1.0, 0.0).astype(bf16)
+        lane = lax.broadcasted_iota(jnp.int32, (8, 2 * n_tok), 1)
+        offset = jnp.where(lane >= n_tok, cap2 // 2, 0)
+        for k, p in enumerate(pairs):
+            loads[k].wait()
+            table = gst[k, :, :, width:].reshape(2 * n_tok, lanes)
+            prob = lax.dot_general(one, table, nt, preferred_element_type=f32)
+            live = prob > 0
+            before = jnp.dot(jnp.where(live, 1.0, 0.0).astype(bf16), earlier, preferred_element_type=f32)
+            prob_v[p] = prob
+            rank_v[p] = jnp.where(live, before.astype(jnp.int32) + offset, -1)
+            pick = jnp.where(taken(p), 1.0, 0.0).astype(bf16)
+
+            def chunk(n, carry, k=k, pick=pick):
+                at = pl.ds(pl.multiple_of(n * step, step), step)
+                got = jnp.dot(pick, gst[k, :, :, at].reshape(2 * n_tok, step), preferred_element_type=f32)
+                rows_v[i, k * cap2 : (k + 1) * cap2, at] = got.astype(bf16)
+                return carry
+
+            lax.fori_loop(0, width // step, chunk, 0)
+
+    def experts(xx, first_i, last_i, first, last):
+        count = last_i + 1 - first_i
+        size = count * 2 * cap2
+        pairs = [pair_of(xx, i, k) for i in range(first_i, last_i + 1) for k in range(2)]
+        weight = jnp.concatenate(
+            [jnp.sum(jnp.where(taken(p), prob_v[p][0:1], 0.0), axis=1, keepdims=True) for p in pairs], axis=0
+        )
+        hidt_v[:, :size] = jnp.concatenate([saved_v[p] for p in pairs], axis=0).T
 
         def chunk(n, carry):
             at = pl.ds(pl.multiple_of(n * step, step), step)
-            rows = jnp.concatenate(
-                [
-                    jnp.dot(
-                        picks[k],
-                        gst[k, :, :, at].reshape(2 * n_tok, step),
-                        preferred_element_type=jnp.float32,
-                    )
-                    for k in range(2)
-                ],
-                axis=0,
-            )
-            proj = lax.dot_general(
-                rows.astype(jnp.bfloat16), w_v[:, at], (((1,), (1,)), ((), ())), preferred_element_type=jnp.float32
-            )
+            rows = rows_v[first_i : last_i + 1, :, at].reshape(size, step)
+            proj = lax.dot_general(rows, w_v[:, at], nt, preferred_element_type=f32)
 
             @pl.when(n == 0)
             def _():
-                proj_v[...] = proj
+                proj_v[:size] = proj
 
             @pl.when(n > 0)
             def _():
-                proj_v[...] += proj
-
-            scaled = (weight * rows).astype(jnp.bfloat16)
-            grad = lax.dot_general(hidden, scaled, (((0,), (0,)), ((), ())), preferred_element_type=jnp.float32)
+                proj_v[:size] += proj
+
+            scaled = (weight * rows.astype(f32)).astype(bf16)
+            grad = jnp.dot(hidt_v[:, :size], scaled, preferred_element_type=f32)
             if not first:
                 grad = acc[:, at] + grad
             if last:
-                gw_v[:, at] = grad.astype(jnp.bfloat16)
+                gw_v[:, at] = grad.astype(bf16)
+                pltpu.make_async_copy(gw_v.at[:, at], gw_ref.at[:, at], gw_sem.at[n]).start()
             else:
                 acc[:, at] = grad
             return carry
 
         lax.fori_loop(0, width // step, chunk, 0)
-        proj = proj_v[...]
-        hid = (weight * proj).astype(jnp.bfloat16)
-        sums = jnp.sum(proj * hidden.astype(jnp.float32), axis=1, keepdims=True)
-        for k, p in enumerate(pairs):
-            hid_v[p] = hid[k * cap2 : (k + 1) * cap2]
-            take = lax.broadcasted_iota(jnp.int32, (cap2, 2 * n_tok), 0) == rank_ref[p]
-            part_ref[p] = jnp.sum(
-                jnp.where(take, sums[k * cap2 : (k + 1) * cap2], 0.0), axis=0, keepdims=True
-            )
+        for j, p in enumerate(pairs):
+            part = slice(j * cap2, (j + 1) * cap2)
+            proj = proj_v[part]
+            hid_v[p] = (weight[part] * proj).astype(bf16)
+            total = jnp.sum(proj * saved_v[p].astype(f32), axis=1, keepdims=True)
+            part_ref[p] = jnp.sum(jnp.where(taken(p), total, 0.0), axis=0, keepdims=True)
 
     def outer(i, first):
         zi = order[i]
@@ -320,38 +336,39 @@
     xo = 1 - x
     z_event(0)
     own_g.wait()
-    own_a.wait()
-    load_w.wait()
-    load_saved.wait()
     for r in range(1, nz):
         z_event(r)
         y_event(r - 1)
         x_event(r - 1)
         if r == nz - 1:
             az_event(0)
-        experts(x, r - 1, r == 1, False)
+        select(x, r - 1)
     y_event(nz - 1)
     x_event(nz - 1)
     az_event(1)
-    experts(x, nz - 1, False, False)
-    experts(xo, 0, False, False)
-    x_event(nz)
-    for i in range(2, nz):
-        az_event(i)
+    select(x, nz - 1)
+    load_w.wait()
+    load_saved.wait()
+    own_a.wait()
+    experts(x, 0, 3, True, False)
+    x_event(4)
+    az_event(2)
+    select(xo, 0)
+    select(xo, 1)
+    az_event(3)
     ay_event(0)
-    experts(xo, 1, False, False)
     outer(0, True)
-    x_event(nz + 1)
     ay_event(1)
     outer(1, False)
-    x_event(nz + 2)
-    experts(xo, 2, False, False)
+    x_event(5)
+    x_event(6)
+    select(xo, 2)
+    experts(xo, 0, 2, False, False)
     ay_event(2)
     outer(2, False)
-    x_event(nz + 3)
-    experts(xo, 3, False, True)
-    out_gw = pltpu.make_async_copy(gw_v, gw_ref, out_sem.at[0])
-    out_gw.start()
+    x_event(7)
+    select(xo, 3)
+    experts(xo, 3, 3, False, True)
     out_hid = pltpu.make_async_copy(hid_v, hid_ref, out_sem.at[1])
     out_hid.start()
     ay_event(3)
@@ -359,7 +376,9 @@
     o_v[...] = oacc[...].astype(jnp.bfloat16)
     out_op = pltpu.make_async_copy(o_v, op_ref, out_sem.at[2])
     out_op.start()
-    out_gw.wait()
+    for n in range(width // step):
+        at = pl.ds(n * step, step)
+        pltpu.make_async_copy(gw_v.at[:, at], gw_ref.at[:, at], gw_sem.at[n]).wait()
     out_hid.wait()
     out_op.wait()
     for op, cond in sends:
@@ -372,12 +391,12 @@
                 op.wait_send()
 
 
-def gather_all(n_tp, n_cp, rows, attn, w_down, saved, rank, prob):
+def gather_all(n_tp, n_cp, rows, attn, w_down, saved):
     nz = n_cp // 2
     dma = pltpu.SemaphoreType.DMA
     n_dev = n_tp * n_cp
-    n_tok, width = rows.shape
-    n_hid = w_down.shape[0]
+    n_tok = rows.shape[0]
+    n_hid, width = w_down.shape
     feat = width // n_cp
     heads = attn.shape[1]
     slots = saved.shape[0] * saved.shape[1]
@@ -395,9 +414,9 @@
             shape(saved.shape, bf16),
             shape(w_down.shape, bf16),
             shape((feat, heads), bf16),
-            shape(prob.shape, f32),
+            shape((n_dev // 2, 1, 2 * n_tok), f32),
         ),
-        in_specs=[hbm] * 4 + [vmem] * 2,
+        in_specs=[hbm] * 4,
         out_specs=[hbm] * 5 + [vmem],
         scratch_shapes=[
             pltpu.VMEM(w_down.shape, bf16),
@@ -405,12 +424,16 @@
             pltpu.VMEM(w_down.shape, f32),
             pltpu.VMEM(w_down.shape, bf16),
             pltpu.VMEM(saved.shape, bf16),
-            pltpu.VMEM((2 * cap2, n_hid), f32),
-            pltpu.VMEM((2, 2, n_tok, width), bf16),
+            pltpu.VMEM((nz * 2 * cap2, n_hid), f32),
+            pltpu.VMEM((2, 2) + rows.shape, bf16),
             pltpu.VMEM((2 * n_tp, n_tok, feat), bf16),
             pltpu.VMEM((2,) + attn.shape, bf16),
             pltpu.VMEM((feat, heads), f32),
             pltpu.VMEM((feat, heads), bf16),
+            pltpu.VMEM((nz, 2 * cap2, width), bf16),
+            pltpu.VMEM((n_hid, nz * 2 * cap2), bf16),
+            pltpu.VMEM((n_dev // 2, 8, 2 * n_tok), jnp.int32),
+            pltpu.VMEM((n_dev // 2, 8, 2 * n_tok), f32),
             dma((nz,)),
             dma((nz,)),
             dma((nz,)),
@@ -426,13 +449,14 @@
             dma((2,)),
             dma((2 * n_tp + 1,)),
             dma((3,)),
+            dma((width // min(1024, width),)),
         ],
         compiler_params=pltpu.CompilerParams(
-            collective_id=0, has_side_effects=True, vmem_limit_bytes=56 * 1024 * 1024
+            collective_id=0, has_side_effects=True, vmem_limit_bytes=60 * 1024 * 1024
         ),
         cost_estimate=pl.CostEstimate(flops=flops, bytes_accessed=4 * n_dev * n_tok * width, transcendentals=0),
         name="gather_and_multiply",
-    )(rows, attn, w_down, saved, rank, prob)
+    )(rows, attn, w_down, saved)
 
 
 def gather_local(grad_out, expert_ids, route_prob, attn_out, w_down, hidden_saved):
@@ -445,18 +469,11 @@
     n_tok, width = rows.shape
     ids = expert_ids[0]
     hit = ids[None] == jnp.arange(n_dev, dtype=jnp.int32)[:, None, None]
-    dense = jnp.sum(jnp.where(hit, route_prob[0].astype(jnp.float32)[None], 0.0), axis=2).astype(jnp.bfloat16)
-    weights = lax.all_to_all(dense, ("tp", "cp"), split_axis=0, concat_axis=0, tiled=True)
-    live = weights > 0
-    earlier = jnp.triu(jnp.ones((n_tok, n_tok), jnp.bfloat16), 1)
-    before = jnp.dot(live.astype(jnp.bfloat16), earlier, preferred_element_type=jnp.float32).astype(jnp.int32)
-    offset = (jnp.arange(n_dev, dtype=jnp.int32) % 2 * cap)[:, None]
-    rank = jnp.where(live, before + offset, -1).reshape(n_dev // 2, 1, 2 * n_tok)
-    prob = weights.astype(jnp.float32).reshape(n_dev // 2, 1, 2 * n_tok)
+    named = ids[:, None, :] == jnp.arange(128, dtype=jnp.int32)[None, :, None]
+    table = jnp.sum(jnp.where(named, route_prob[0].astype(jnp.float32)[:, None, :], 0.0), axis=2)
+    rows = jnp.concatenate([rows, table.astype(jnp.bfloat16)], axis=1)
     saved = hidden_saved[0].reshape(n_dev // 2, 2 * cap, hidden_saved.shape[2])
-    _, _, hid, grad_w, grad_oproj, part = gather_all(
-        n_tp, n_cp, rows, attn_out, w_down[0], saved, rank, prob
-    )
+    _, _, hid, grad_w, grad_oproj, part = gather_all(n_tp, n_cp, rows, attn_out, w_down[0], saved)
     returned = lax.all_to_all(part.reshape(n_dev, n_tok), ("tp", "cp"), split_axis=0, concat_axis=0, tiled=True)
     grad_prob = jnp.sum(jnp.where(hit, returned[:, :, None], 0.0), axis=0)[None]
     return (grad_prob, hid.reshape(hidden_saved.shape), grad_w[None], grad_oproj)

time: 309 us -> 259 us (0.84)
  Pallas kernels: 270 us -> 233 us
  waiting for transfers between devices: 14.1 us -> 7.1 us
  starting transfers between devices: 9.77 us -> 2.81 us
    pallas_call x1, Pallas kernels: 270 us -> 233 us  [gather_all(): pl.pallas_call(functools.partial(gather_kernel, n_tp, n_cp), out_shape=(s...]
    all_to_all x1 -> x0, starting transfers between devices: 7.3 us -> none  [gather_local(): lax.all_to_all(dense, ('tp', 'cp'), split_axis=0, concat_axis=0, tiled=True)]
    all_to_all x1 -> x0, waiting for transfers between devices: 7.03 us -> none  [gather_local(): lax.all_to_all(dense, ('tp', 'cp'), split_axis=0, concat_axis=0, tiled=True)]
  transfers between devices with their start and end apart: 2 -> 1, of which waited for: 2 -> 1; matrix products, arithmetic and copies ran while one was open for 0% -> 0% of each run, Pallas kernels for 0% -> 0%
where the time goes in v3:
time: 259 us
  Pallas kernels  233 us (90%)
  local copies, waits for them, and re-layouts  11.2 us (4%)
  waiting for transfers between devices  7.1 us (3%)
  other arithmetic  3.96 us (2%)
  starting transfers between devices  2.81 us (1%)
    pallas_call x1, Pallas kernels, gather_all(): pl.pallas_call(functools.partial(gather_kernel, n_tp, n_cp), out_shape=(s...  233 us
    unnamed x7, local copies, waits for them, and re-layouts  10.3 us
    all_to_all x1, waiting for transfers between devices, gather_local(): lax.all_to_all(part.reshape(n_dev, n_tok), ('tp', 'cp'), split_axis=0, co...  7.1 us
  transfers between devices with their start and end apart: 1, of which 1 were waited for; matrix products, arithmetic and copies ran while one was open for 0% of the time, Pallas kernels for 0%

profile of v3, /device:TPU:0, one launch (start us, length us, event | category | flops | bytes accessed | tf_op | source)
XLA Modules:
  0.0 258.6 jit_solution(10042470607452960579)
XLA Ops:
  0.6 0.7 bitcast_convert_fusion
  1.3 0.1 copy.18
  1.4 0.8 copy.17
  2.2 0.4 select_reduce_fusion
  2.6 2.3 pad_maximum_fusion.g_ref
  4.9 0.0 copy-start.1
  4.9 232.8 %gather_and_multiply.1 = (bf16[32,128,4224]{2,1,0:T(8,128)(2,1)}, bf16[8,512,1024]{2,1,0:T(8,128)(2,1)}, bf16[16,80,768]{2,1,0:T(8,128)(2,1)}, bf16[768,4096]{1,...) custom-call(bf16[128,4224]{1,0:T(8,128)(2,1)} %pad_maximum_fusion.g_ref, bf16[512,1024]{1,0:T(8,128)(2,1)} %a_ref.1, ...), custom_call_target="tpu_custom_call" | custom-call | flops 20401094656 | bytes 67108864 | tf_op jit(solution)/shard_map/gather_and_multiply/pallas_call | solution.py:409
  237.7 2.8 %all-to-all-start = ((f32[32,1,128]{2,1,0:T(1,128)}), f32[32,1,128]{2,1,0:T(1,128)S(1)}, u32[]{:S(2)}, u32[]{:S(2)}) async-start(f32[32,1,128]{2,1,0:T(1,128)} %bitcast.18), calls=%async_computation | async-start | bytes 32768 | tf_op jit(solution)/shard_map/all_to_all | solution.py:477
  240.5 7.1 %all-to-all-done = f32[32,1,128]{2,1,0:T(1,128)S(1)} async-done(((f32[32,1,128]{2,1,0:T(1,128)}), f32[32,1,128]{2,1,0:T(1,128)S(1)}, u32[]{:S(2)}, u32[]{:S(2)}) %all-to-all-start) | async-done | bytes 16416 | tf_op jit(solution)/shard_map/all_to_all | solution.py:477
  247.6 0.0 copy-done.1
  247.6 0.6 select_reduce_fusion.1
  248.3 2.9 %copy.23 = bf16[1,1280,768]{2,1,0:T(8,128)(2,1)} copy(bf16[1,1280,768]{2,1,0:T(8,128)(2,1)} %bitcast.15) | data formatting | bytes 3932160
  251.2 0.0 copy-start
  251.2 6.4 %copy.24 = bf16[1,768,4096]{2,1,0:T(8,128)(2,1)} copy(bf16[1,768,4096]{2,1,0:T(8,128)(2,1)} %bitcast.14) | data formatting | bytes 12582912
  257.6 0.0 copy-done
  257.6 1.0 copy.25
Async XLA Ops:
  4.9 242.8 %copy-start.1 = (s32[1,128,8]{1,2,0:T(8,128)S(1)}, s32[1,128,8]{1,2,0:T(8,128)}, u32[]{:S(2)}) copy-start(s32[1,128,8]{1,2,0:T(8,128)} %param.7) | copy-start | bytes 12292
  237.7 9.9 %all-to-all-start = ((f32[32,1,128]{2,1,0:T(1,128)}), f32[32,1,128]{2,1,0:T(1,128)S(1)}, u32[]{:S(2)}, u32[]{:S(2)}) async-start(f32[32,1,128]{2,1,0:T(1,128)} %bitcast.18), calls=%async_computation | async-start | bytes 32768 | tf_op jit(solution)/shard_map/all_to_all | solution.py:477
  251.2 6.4 %copy-start = (bf16[512,1024]{1,0:T(8,128)(2,1)S(1)}, bf16[512,1024]{1,0:T(8,128)(2,1)}, u32[]{:S(2)}) copy-start(bf16[512,1024]{1,0:T(8,128)(2,1)} %get-tuple-element.19) | copy-start | bytes 3145732

commit v4 on v3

--- a/solution.py
+++ b/solution.py
@@ -355,15 +355,16 @@
     az_event(2)
     select(xo, 0)
     select(xo, 1)
-    az_event(3)
     ay_event(0)
     outer(0, True)
+    az_event(3)
+    experts(xo, 0, 1, False, False)
     ay_event(1)
     outer(1, False)
     x_event(5)
     x_event(6)
     select(xo, 2)
-    experts(xo, 0, 2, False, False)
+    experts(xo, 2, 2, False, False)
     ay_event(2)
     outer(2, False)
     x_event(7)
@@ -459,6 +460,30 @@
     )(rows, attn, w_down, saved)
 
 
+def place_kernel(*refs):
+    n = (len(refs) - 1) // 2
+    copies = [pltpu.make_async_copy(refs[k], refs[n + k], refs[-1].at[k]) for k in range(n)]
+    for copy in copies:
+        copy.start()
+    for copy in copies:
+        copy.wait()
+
+
+def place_results(*values):
+    hbm = pl.BlockSpec(memory_space=pl.ANY)
+    return pl.pallas_call(
+        place_kernel,
+        out_shape=tuple(jax.ShapeDtypeStruct(v.shape, v.dtype) for v in values),
+        in_specs=[hbm] * len(values),
+        out_specs=[hbm] * len(values),
+        scratch_shapes=[pltpu.SemaphoreType.DMA((len(values),))],
+        cost_estimate=pl.CostEstimate(
+            flops=0, bytes_accessed=sum(2 * v.size * v.dtype.itemsize for v in values), transcendentals=0
+        ),
+        name="place_results",
+    )(*values)
+
+
 def gather_local(grad_out, expert_ids, route_prob, attn_out, w_down, hidden_saved):
     n_tp = lax.axis_size("tp")
     n_cp = lax.axis_size("cp")
@@ -476,6 +501,7 @@
     _, _, hid, grad_w, grad_oproj, part = gather_all(n_tp, n_cp, rows, attn_out, w_down[0], saved)
     returned = lax.all_to_all(part.reshape(n_dev, n_tok), ("tp", "cp"), split_axis=0, concat_axis=0, tiled=True)
     grad_prob = jnp.sum(jnp.where(hit, returned[:, :, None], 0.0), axis=0)[None]
+    hid, grad_w, grad_oproj = place_results(hid, grad_w, grad_oproj)
     return (grad_prob, hid.reshape(hidden_saved.shape), grad_w[None], grad_oproj)
 
 

time: 259 us -> 527 us (2.03)
  Pallas kernels: 233 us -> 518 us
  local copies, waits for them, and re-layouts: 11.2 us -> 0.9 us
  waiting for transfers between devices: 7.1 us -> 0.01 us
    pallas_call x0 -> x1, Pallas kernels: none -> 283 us  [place_results(): pl.pallas_call(place_kernel, out_shape=tuple((jax.ShapeDtypeStruct(v.shap...]
    unnamed x7 -> x2, local copies, waits for them, and re-layouts: 10.3 us -> 0.01 us
    all_to_all x1, waiting for transfers between devices: 7.1 us -> 0.01 us  [gather_local(): lax.all_to_all(part.reshape(n_dev, n_tok), ('tp', 'cp'), split_axis=0, co...]
  transfers between devices with their start and end apart: 1 -> 1, of which waited for: 1 -> 0; matrix products, arithmetic and copies ran while one was open for 0% -> 0% of each run, Pallas kernels for 0% -> 54%
where the time goes in v4:
time: 527 us
  Pallas kernels  518 us (98%)
    pallas_call x1, Pallas kernels, place_results(): pl.pallas_call(place_kernel, out_shape=tuple((jax.ShapeDtypeStruct(v.shap...  283 us
    pallas_call x1, Pallas kernels, gather_all(): pl.pallas_call(functools.partial(gather_kernel, n_tp, n_cp), out_shape=(s...  235 us
  transfers between devices with their start and end apart: 1, of which 0 were waited for; matrix products, arithmetic and copies ran while one was open for 0% of the time, Pallas kernels for 54%

profile of v4, /device:TPU:0, one launch (start us, length us, event | category | flops | bytes accessed | tf_op | source)
XLA Modules:
  0.0 526.5 jit_solution(18057979723220950296)
XLA Ops:
  0.6 0.7 bitcast_convert_fusion
  1.3 0.1 copy.18
  1.4 0.8 copy.17
  2.2 0.4 select_reduce_fusion
  2.6 2.3 pad_maximum_fusion.g_ref
  4.9 235.1 %gather_and_multiply.1 = (bf16[32,128,4224]{2,1,0:T(8,128)(2,1)}, bf16[8,512,1024]{2,1,0:T(8,128)(2,1)}, bf16[16,80,768]{2,1,0:T(8,128)(2,1)}, bf16[768,4096]{1,...) custom-call(bf16[128,4224]{1,0:T(8,128)(2,1)} %pad_maximum_fusion.g_ref, bf16[512,1024]{1,0:T(8,128)(2,1)} %a_ref.1, ...), custom_call_target="tpu_custom_call" | custom-call | flops 20401094656 | bytes 67108864 | tf_op jit(solution)/shard_map/gather_and_multiply/pallas_call | solution.py:410
  240.0 2.8 all-to-all-start
  242.8 0.0 copy-start
  242.9 283.0 %place_results.1 = (bf16[16,80,768]{2,1,0:T(8,128)(2,1)}, bf16[768,4096]{1,0:T(8,128)(2,1)}, bf16[512,1024]{1,0:T(8,128)(2,1)}) custom-call(bf16[16,80,768]{2,1,0:T(8,128)(2,1)} %get-tuple-element.12.refs_0_, bf16[768,4096]{1,0:T(8,128)(2,1)} %get-tuple-element.13.refs_1_, bf16[512,1024]{1,0:T(8,128)(2,1)} %get-tuple-element.14.refs_2_), custom_call_target="tpu_custom_call" | custom-call | bytes 18612224 | tf_op jit(solution)/shard_map/place_results/pallas_call | solution.py:474
  525.9 0.0 all-to-all-done
  525.9 0.0 copy-done
  525.9 0.6 select_reduce_fusion.1
Async XLA Ops:
  240.0 285.9 %all-to-all-start = ((f32[32,1,128]{2,1,0:T(1,128)}), f32[32,1,128]{2,1,0:T(1,128)S(1)}, u32[]{:S(2)}, u32[]{:S(2)}) async-start(f32[32,1,128]{2,1,0:T(1,128)} %bitcast.16), calls=%async_computation | async-start | bytes 32768 | tf_op jit(solution)/shard_map/all_to_all | solution.py:502
  242.8 283.1 %copy-start = (s32[1,128,8]{1,2,0:T(8,128)S(1)}, s32[1,128,8]{1,2,0:T(8,128)}, u32[]{:S(2)}) copy-start(s32[1,128,8]{1,2,0:T(8,128)} %param.7) | copy-start | bytes 12292
